TPU v7x, 128 devices: a whole 4x4x4 slice. The times are simulated.
128 devices in a mesh: wide: 32 (over y, z, core), narrow: 4 (over x).
Axes of the slice: x: 4, y: 4, z: 4, core: 2. Of those that a mesh axis runs over, the one named last changes fastest.
Arguments:
- superheat_excess: float32 [128, 512, 512], P('wide', 'narrow'), may hold values from -6 to 6
- liquid_indicator: int32 [128, 512, 512], P('wide', 'narrow'), may hold values from 0 to 1, as said below
- group_patch_listing_table: int32 [32, 4, 16], P('wide', 'narrow'), may hold values from -1 to 31, as said below
- source_smearing_factors_north: float32 [16, 16], replicated, may hold values from 0 to 2, as said below
- source_smearing_factors_east: float32 [128, 128], replicated, may hold values from 0 to 2, as said below
Outputs:
- temperature_next: float32 [128, 512, 512], P('wide', 'narrow')
- pressure: float32 [128, 512, 512], P('wide', 'narrow')
- residual: float32 [128, 512, 512], P('wide', 'narrow')
Inputs may be any that keep to these rules, and one draw needn't show every extreme that they name: In each row group_patch_listing_table[w, n] the listed tile numbers come first and are distinct, the remaining entries are -1. A row lists 1 to 16 tiles; for every w the rows n < 4 list exactly 32 tiles together, and one of them lists 16. `liquid_indicator`: phase is 1 in every cell outside the listed tiles. `source_smearing_factors_north`: the identity plus entries drawn in 0 to 1.2 / 16. `source_smearing_factors_east`: the identity plus entries drawn in 0 to 1.2 / 128.
All inputs are finite; a program needn't handle non-finite values.
Results may differ from a plain program's by a relative error of at most 0.0003.
Values sent between devices are 32-bit elements; how exact they have to be, the bound alone decides.
A program may use at most 64 MiB of HBM per device.

v0:
```python
import math
import jax
import jax.numpy as jnp
from jax import lax
from jax.sharding import Mesh
from jax.sharding import PartitionSpec as P

ITERS = 3
WIDE_NARROW = ("wide_0", "wide_1", "wide_2", "narrow")
WIDE = ("wide_0", "wide_1", "wide_2")
conduct_liquid = 1.0
conduct_vapor = 0.4
diffusion = 0.06
mobility_liquid = 1.0
mobility_vapor = 4.0
expansion = 0.3
compress = 0.01
highest = lax.Precision.HIGHEST


def padded_2(array, sides, width):
    edges = {}
    for axis, dim in sides:
        devices, length = (lax.axis_size(axis), array.shape[dim])
        up = [(i, (i + 1) % devices) for i in range(devices - 1)]
        last = lax.slice_in_dim(array, length - width, length, axis=dim)
        initial = lax.slice_in_dim(array, 0, width, axis=dim)
        edges[dim] = (
            lax.ppermute(last, axis, up),
            lax.ppermute(initial, axis, [(b, a) for a, b in up]),
        )
    done = []
    for _, dim in sides:
        low, high = edges[dim]
        around = [(width, width) if d in done else (0, 0) for d in range(array.ndim)]
        array = jnp.concatenate([jnp.pad(low, around), array, jnp.pad(high, around)], axis=dim)
        done.append(dim)
    return array


def over_axes(array, axes):
    for axis in axes:
        array = lax.psum(array, axis)
    return array


def centre(padded):
    return padded[1:-1, 1:-1, 1:-1]


def neighbours(padded):
    return [
        padded[2:, 1:-1, 1:-1],
        padded[:-2, 1:-1, 1:-1],
        padded[1:-1, 2:, 1:-1],
        padded[1:-1, :-2, 1:-1],
        padded[1:-1, 1:-1, 2:],
        padded[1:-1, 1:-1, :-2],
    ]


def heat_advance(temp_pad, liquid_indicator_haloed, inner_region_haloed):
    current = centre(temp_pad)
    phases = centre(liquid_indicator_haloed)
    conduct = jnp.where(phases > 0.5, conduct_liquid, conduct_vapor)
    flux = jnp.zeros_like(current)
    faces = jnp.zeros_like(current)
    for near_temp, near_phase, near_inside in zip(
        neighbours(temp_pad), neighbours(liquid_indicator_haloed), neighbours(inner_region_haloed)
    ):
        differ = jnp.abs(near_phase - phases) > 0.5
        flux = flux + near_inside * jnp.where(differ, -2.0 * current, near_temp - current)
        faces = faces + near_inside * jnp.where(differ, 1.0, 0.0)
    heated_values = current + diffusion * conduct * flux
    vaporised_amount = 2.0 * conduct * faces * heated_values
    return (heated_values, vaporised_amount)


def face_weights(liquid_indicator_haloed, inner_region_haloed):
    mobility = jnp.where(liquid_indicator_haloed > 0.5, mobility_liquid, mobility_vapor)
    own = centre(mobility)
    return [
        near_inside * 0.5 * (own + near_mob)
        for near_inside, near_mob in zip(neighbours(inner_region_haloed), neighbours(mobility))
    ]


def apply_operator(field_pad, weights):
    field = centre(field_pad)
    total = compress * field
    for weight, near in zip(weights, neighbours(field_pad)):
        total = total + weight * (field - near)
    return total


def smear_tiles(tiles, source_smearing_factors_north, source_smearing_factors_east):
    across = jnp.einsum("...bc,dc->...bd", tiles, source_smearing_factors_east, precision=highest)
    return expansion * jnp.einsum(
        "ab,...bd->...ad", source_smearing_factors_north, across, precision=highest
    )


def cosine_rows(extent, klength, clength):
    waves = jnp.arange(klength, dtype=jnp.int32)
    centres = 2 * jnp.arange(clength, dtype=jnp.int32) + 1
    turns = waves[:, None] * centres[None, :] % (4 * extent)
    angles = 2.0 * math.pi / (4 * extent) * turns.astype(jnp.float32)
    scales = jnp.where(waves == 0, math.sqrt(1.0 / extent), math.sqrt(2.0 / extent)).astype(
        jnp.float32
    )
    return scales[:, None] * jnp.cos(angles)


def eigen(extent, first, length):
    waves = (first + jnp.arange(length, dtype=jnp.int32)).astype(jnp.float32)
    return 4.0 * jnp.sin(waves * (math.pi / (2 * extent))) ** 2


def inside_range(first, length, limit):
    places = first + jnp.arange(length, dtype=jnp.int32)
    return jnp.logical_and(places >= 0, places < limit).astype(jnp.float32)


def padded_field(field):
    rimmed = padded_2(field, ((WIDE, 0), ("narrow", 1)), 1)
    return jnp.pad(rimmed, ((0, 0), (0, 0), (1, 1)))


def inner(first_field, second_field):
    return over_axes(jnp.sum(first_field * second_field), WIDE_NARROW)


def on_device(
    superheat_excess,
    liquid_indicator,
    group_patch_listing_table,
    source_smearing_factors_north,
    source_smearing_factors_east,
):
    sheet_thickness, north_line_total, patch_span_east = superheat_excess.shape
    wide_count = lax.axis_size(WIDE)
    lanes = lax.axis_size("narrow")
    wide_index = lax.axis_index(WIDE)
    lane_index = lax.axis_index("narrow")
    total_y = north_line_total * lanes
    total_z = sheet_thickness * wide_count
    gathered_patches = jnp.stack([superheat_excess, liquid_indicator.astype(jnp.float32)])
    rimmed = padded_2(gathered_patches, ((WIDE, 1), ("narrow", 2)), 1)
    rimmed = jnp.pad(rimmed, ((0, 0), (0, 0), (0, 0), (1, 1)))
    z_inside = inside_range(wide_index * sheet_thickness - 1, sheet_thickness + 2, total_z)
    y_inside = inside_range(lane_index * north_line_total - 1, north_line_total + 2, total_y)
    x_inside = inside_range(-1, patch_span_east + 2, patch_span_east)
    inner_region_haloed = (
        z_inside[:, None, None] * y_inside[None, :, None] * x_inside[None, None, :]
    )
    heated_values, vaporised_amount = heat_advance(rimmed[0], rimmed[1], inner_region_haloed)
    flat_ids = group_patch_listing_table.reshape(-1)
    most = flat_ids.shape[0]
    size_y = source_smearing_factors_north.shape[0]
    size_x = source_smearing_factors_east.shape[0]
    tiles_y = north_line_total // size_y
    tiles_x = patch_span_east // size_x
    count_tiles = tiles_y * tiles_x
    blocks = vaporised_amount.reshape(sheet_thickness, tiles_y, size_y, tiles_x, size_x).transpose(
        1, 3, 0, 2, 4
    )
    blocks = blocks.reshape(count_tiles, sheet_thickness * size_y * size_x)
    listed = flat_ids >= 0
    numbers = jnp.arange(count_tiles, dtype=jnp.int32)
    choose = jnp.logical_and(flat_ids[:, None] == numbers[None, :], listed[:, None]).astype(
        jnp.float32
    )
    picked = jnp.dot(choose, blocks, precision=highest)
    smeared = smear_tiles(
        picked.reshape(most, sheet_thickness, size_y, size_x),
        source_smearing_factors_north,
        source_smearing_factors_east,
    ).reshape(most, -1)
    sourced = jnp.dot(choose.T, smeared, precision=highest)
    source = sourced.reshape(tiles_y, tiles_x, sheet_thickness, size_y, size_x).transpose(
        2, 0, 3, 1, 4
    )
    source = source.reshape(sheet_thickness, north_line_total, patch_span_east)
    table_x = cosine_rows(patch_span_east, patch_span_east, patch_span_east)
    table_z = cosine_rows(total_z, total_z, total_z)
    eigen_z = eigen(total_z, 0, total_z)
    table_y = cosine_rows(total_y, total_y, total_y).reshape(total_y, lanes, north_line_total)
    table_zw = table_z.reshape(total_z, wide_count, sheet_thickness)
    part_k = patch_span_east // (wide_count * lanes)
    eigen_y = eigen(total_y, 0, total_y)
    eigen_x = eigen(patch_span_east, (wide_index * lanes + lane_index) * part_k, part_k)

    def precondition(remainder):
        spectrum = jnp.einsum("zyx,kx->zyk", remainder, table_x, precision=highest)
        planes = lax.all_to_all(
            spectrum[None], WIDE_NARROW, split_axis=3, concat_axis=0, tiled=True
        )
        planes = planes.reshape(wide_count, lanes, sheet_thickness, north_line_total, part_k)
        planes = jnp.einsum("wnzyk,mwz->mnyk", planes, table_zw, precision=highest)
        planes = jnp.einsum("mnyk,lny->mlk", planes, table_y, precision=highest)
        denom = eigen_z[:, None, None] + eigen_y[None, :, None] + eigen_x[None, None, :] + compress
        planes = jnp.einsum("mlk,lny->mnyk", planes / denom, table_y, precision=highest)
        planes = jnp.einsum("mnyk,mwz->wnzyk", planes, table_zw, precision=highest)
        planes = planes.reshape(wide_count * lanes, sheet_thickness, north_line_total, part_k)
        slabs = lax.all_to_all(planes, WIDE_NARROW, split_axis=0, concat_axis=3, tiled=True)
        return jnp.einsum("zyk,kx->zyx", slabs[0], table_x, precision=highest)

    weights = face_weights(rimmed[1], inner_region_haloed)
    pressure = jnp.zeros_like(source)
    residual = source
    search = precondition(residual)
    aligned = inner(residual, search)
    direction = search
    for iteration in range(ITERS):
        image = apply_operator(padded_field(direction), weights)
        alpha = aligned / over_axes(jnp.sum(direction * image), WIDE_NARROW)
        pressure = pressure + alpha * direction
        residual = residual - alpha * image
        if iteration + 1 < ITERS:
            search = precondition(residual)
            renewed = inner(residual, search)
            direction = search + renewed / aligned * direction
            aligned = renewed
    return (heated_values, pressure, residual)


def solution(mesh):
    torus = Mesh(
        mesh.devices.reshape(4, 4, 2, mesh.shape["narrow"]),
        ("wide_0", "wide_1", "wide_2", "narrow"),
    )
    placed = (P(WIDE, "narrow", None), P(WIDE, "narrow", None), P(WIDE, "narrow", None), P(), P())
    return jax.shard_map(
        on_device,
        mesh=torus,
        in_specs=placed,
        out_specs=(P(WIDE, "narrow", None), P(WIDE, "narrow", None), P(WIDE, "narrow", None)),
        check_vma=False,
    )
```

profile of v0, /device:TPU:34, one launch (start us, length us, event | category | flops | bytes accessed | tf_op | source)
XLA Modules:
  0.0 524.9 jit_solution(13043440437132954281)
XLA Ops:
  2.3 3.4 collective-permute-start
  11.1 3.6 collective-permute-start.2
  15.1 4.8 collective-permute-done.1
  27.2 4.9 fusion.6
  44.3 7.0 %convolution_bitcast_fusion.15 = f32[1,4,128,512]{3,2,1,0:T(8,128)} fusion(f32[4,128,512]{2,1,0:T(8,128)S(1)} %reshape.309, s32[512]{0:T(512)S(1)} %multiply_add_fusion.3, f32[512]{0:T(512)S(1)} %fusion.261), kind=kOutput, calls=%fused_computation.47 | convolution fusion | flops 1614544896 | bytes 2101248 | tf_op jit(solution)/shard_map/zyx,kx->zyk/dot_general | solution.py:194
  53.9 12.1 %all-to-all-start = ((f32[1,4,128,512]{2,1,0,3:T(4,128)}), f32[1,4,128,512]{2,1,0,3:T(4,128)S(1)}, u32[]{:S(2)}, u32[]{:S(2)}) async-start(f32[1,4,128,512]{2,1,0,3:T(4,128)} %copy.65), calls=%async_computation | async-start | bytes 2097152 | tf_op jit(solution)/shard_map/all_to_all | solution.py:195
  66.3 17.5 %all-to-all-done = f32[1,4,128,512]{2,1,0,3:T(4,128)S(1)} async-done(((f32[1,4,128,512]{2,1,0,3:T(4,128)}), f32[1,4,128,512]{2,1,0,3:T(4,128)S(1)}, u32[]{:S(2)}, u32[]{:S(2)}) %all-to-all-start) | async-done | bytes 1048608 | tf_op jit(solution)/shard_map/all_to_all | solution.py:195
  85.4 7.2 %convolution_bitcast_fusion.13 = f32[128,512,4]{0,1,2:T(8,128)S(1)} fusion(f32[128,4,128,4]{2,0,1,3:T(8,128)S(1)} %convolution_bitcast_fusion.14, s32[4,128]{1,0:T(4,128)S(1)} %multiply_add_fusion.4, f32[512]{0:T(512)S(1)} %fusion.261), kind=kOutput, calls=%fused_computation.45 | convolution fusion | flops 1614544896 | bytes 2101248 | tf_op jit(solution)/shard_map/mnyk,lny->mlk/dot_general | solution.py:200
  92.7 6.3 %convolution_bitcast_fusion.12 = f32[128,4,128,4,1]{0,2,3,1,4:T(8,128)S(1)} fusion(f32[128,512,4]{0,1,2:T(8,128)S(1)} %convolution_bitcast_fusion.13, f32[4]{0:T(128)S(1)} %multiply_multiply_fusion.1, f32[128,512]{0,1:T(8,128)S(1)} %broadcast_add_fusion, s32[4,128]{1,0:T(4,128)S(1)} %multiply_add_fusion.4, f32[512]{0:T(512)S(1)} %fusion.261), kind=kOutput, calls=%fused_computation.44 | convolution fusion | flops 1615331328 | bytes 2363408 | tf_op jit(solution)/shard_map/mlk,lny->mnyk/dot_general | solution.py:202
  101.7 23.1 %all_to_all.90 = f32[128,4,128,4]{2,3,1,0:T(4,128)S(1)} all-to-all(f32[128,4,128,4]{2,3,1,0:T(4,128)S(1)} %copy.74), channel_id=1, replica_groups=mesh['wide_0'=4,'wide_1'=4,'wide_2'=2,'narrow'=4] {'wide_0','wide_1','wi..., dimensions={0} | all-to-all | bytes 2097152 | tf_op jit(solution)/shard_map/all_to_all | solution.py:205
  125.0 5.8 %fusion.126 = f32[4,128,512]{2,1,0:T(8,128)S(1)} fusion(f32[4,128,512]{1,2,0:T(8,128)S(1)} %bitcast.221, s32[512]{0:T(512)S(1)} %multiply_add_fusion.3, f32[512]{0:T(512)S(1)} %fusion.261), kind=kOutput, calls=%fused_computation.235 | convolution fusion | flops 1614544896 | bytes 2101248 | tf_op jit(solution)/shard_map/zyk,kx->zyx/dot_general | solution.py:206
  132.8 3.6 collective-permute-start.4
  138.6 3.7 collective-permute-start.6
  144.9 7.6 %multiply_reduce_fusion.4 = (f32[]{:T(128)}, f32[]{:T(128)}, f32[4,128,512]{2,1,0:T(8,128)}, f32[4,128,512]{2,1,0:T(8,128)}, f32[4,128,512]{2,1,0:T(8,128)}, /*i...) fusion(f32[4,128,512]{2,1,0:T(8,128)S(1)} %fusion.126, ...), kind=kLoop, calls=%fused_computation.222 | loop fusion | flops 12845054 | bytes 25714696 | tf_op jit(solution)/shard_map/reduce_sum | solution.py:216
  152.5 9.3 %all-reduce.14 = (f32[]{:T(128)}, f32[]{:T(128)}) all-reduce(f32[]{:T(128)} %get-tuple-element.4, f32[]{:T(128)} %get-tuple-element.3), channel_id=1, replica_groups=mesh['wide_0'=4,'wide_1'=4,'wide_2'=2,'narrow'=4] {'wide_0'}, use_global_device_ids=true, to_apply=%region_1.2 | all-reduce | flops 2 | bytes 16 | tf_op jit(solution)/shard_map/psum | solution.py:43
  161.8 12.1 %all-reduce.13 = (f32[]{:T(128)}, f32[]{:T(128)}) all-reduce(f32[]{:T(128)} %get-tuple-element.9, f32[]{:T(128)} %get-tuple-element.10), channel_id=1, replica_groups=mesh['wide_0'=4,'wide_1'=4,'wide_2'=2,'narrow'=4] {'wide_1'}, use_global_device_ids=true, to_apply=%region_2.3 | all-reduce | flops 2 | bytes 16 | tf_op jit(solution)/shard_map/psum | solution.py:43
  173.9 3.1 all-reduce.15
  177.0 10.0 %all-reduce.12 = (f32[]{:T(128)}, f32[]{:T(128)}) all-reduce(f32[]{:T(128)} %get-tuple-element.11, f32[]{:T(128)} %get-tuple-element.12), channel_id=1, replica_groups=mesh['wide_0'=4,'wide_1'=4,'wide_2'=2,'narrow'=4] {'narrow'}, use_global_device_ids=true, to_apply=%region_4.5 | all-reduce | flops 2 | bytes 16 | tf_op jit(solution)/shard_map/psum | solution.py:43
  190.0 6.8 %convolution_bitcast_fusion.10 = f32[1,4,128,512]{3,2,1,0:T(8,128)} fusion(f32[4,128,512]{2,1,0:T(8,128)S(1)} %multiply_subtract_fusion.2, s32[512]{0:T(512)S(1)} %multiply_add_fusion.3, f32[512]{0:T(512)S(1)} %fusion.261), kind=kOutput, calls=%fused_computation.42 | convolution fusion | flops 1614544896 | bytes 2101248 | tf_op jit(solution)/shard_map/zyx,kx->zyk/dot_general | solution.py:194
  198.4 21.8 %all_to_all.91 = f32[1,4,128,512]{2,1,0,3:T(4,128)S(1)} all-to-all(f32[1,4,128,512]{2,1,0,3:T(4,128)S(1)} %copy.77), channel_id=1, replica_groups=mesh['wide_0'=4,'wide_1'=4,'wide_2'=2,'narrow'=4] {'wide_0','wide_1','wi..., dimensions={3} | all-to-all | bytes 2097152 | tf_op jit(solution)/shard_map/all_to_all | solution.py:195
  221.9 7.2 %convolution_bitcast_fusion.8 = f32[128,512,4]{0,1,2:T(8,128)S(1)} fusion(f32[128,4,128,4]{2,0,1,3:T(8,128)S(1)} %convolution_bitcast_fusion.9, s32[4,128]{1,0:T(4,128)S(1)} %multiply_add_fusion.4, f32[512]{0:T(512)S(1)} %fusion.261), kind=kOutput, calls=%fused_computation.40 | convolution fusion | flops 1614544896 | bytes 2101248 | tf_op jit(solution)/shard_map/mnyk,lny->mlk/dot_general | solution.py:200
  229.2 6.0 %convolution_bitcast_fusion.7 = f32[128,4,128,4,1]{0,2,3,1,4:T(8,128)S(1)} fusion(f32[128,512,4]{0,1,2:T(8,128)S(1)} %convolution_bitcast_fusion.8, f32[4]{0:T(128)S(1)} %multiply_multiply_fusion.1, f32[128,512]{0,1:T(8,128)S(1)} %broadcast_add_fusion, s32[4,128]{1,0:T(4,128)S(1)} %multiply_add_fusion.4, f32[512]{0:T(512)S(1)} %fusion.261), kind=kOutput, calls=%fused_computation.39 | convolution fusion | flops 1615331328 | bytes 2363408 | tf_op jit(solution)/shard_map/mlk,lny->mnyk/dot_general | solution.py:202
  237.9 22.9 %all_to_all.92 = f32[128,4,128,4]{2,3,1,0:T(4,128)S(1)} all-to-all(f32[128,4,128,4]{2,3,1,0:T(4,128)S(1)} %copy.86), channel_id=1, replica_groups=mesh['wide_0'=4,'wide_1'=4,'wide_2'=2,'narrow'=4] {'wide_0','wide_1','wi..., dimensions={0} | all-to-all | bytes 2097152 | tf_op jit(solution)/shard_map/all_to_all | solution.py:205
  261.1 6.6 %multiply_reduce_fusion.3 = (f32[]{:T(128)}, f32[4,128,512]{2,1,0:T(8,128)S(1)}) fusion(f32[4,128,512]{2,1,0:T(8,128)S(1)} %multiply_subtract_fusion.2, f32[4,128,512]{1,2,0:T(8,128)S(1)} %bitcast.220, s32[512]{0:T(512)S(1)} %multiply_add_fusion.3, f32[512]{0:T(512)S(1)} %fusion.261), kind=kOutput, calls=%fused_computation.219 | convolution fusion | flops 1615069184 | bytes 3149828 | tf_op jit(solution)/shard_map/zyk,kx->zyx/dot_general | solution.py:206
  267.6 9.4 %psum.176 = f32[]{:T(128)} all-reduce(f32[]{:T(128)} %get-tuple-element.51), channel_id=1, replica_groups=mesh['wide_0'=4,'wide_1'=4,'wide_2'=2,'narrow'=4] {'wide_0'}, use_global_device_ids=true, to_apply=%region_11.12 | all-reduce | flops 1 | bytes 8 | tf_op jit(solution)/shard_map/psum | solution.py:43
  277.1 9.5 %psum.177 = f32[]{:T(128)} all-reduce(f32[]{:T(128)} %psum.176), channel_id=1, replica_groups=mesh['wide_0'=4,'wide_1'=4,'wide_2'=2,'narrow'=4] {'wide_1'}, use_global_device_ids=true, to_apply=%region_12.13 | all-reduce | flops 1 | bytes 8 | tf_op jit(solution)/shard_map/psum | solution.py:43
  289.7 9.8 %psum.179 = f32[]{:T(128)} all-reduce(f32[]{:T(128)} %psum.178), channel_id=1, replica_groups=mesh['wide_0'=4,'wide_1'=4,'wide_2'=2,'narrow'=4] {'narrow'}, use_global_device_ids=true, to_apply=%region_14.15 | all-reduce | flops 1 | bytes 8 | tf_op jit(solution)/shard_map/psum | solution.py:43
  303.2 3.6 collective-permute-start.8
  309.2 3.5 collective-permute-start.10
  317.8 9.3 %psum.180 = f32[]{:T(128)} all-reduce(f32[]{:T(128)} %get-tuple-element.15), channel_id=1, replica_groups=mesh['wide_0'=4,'wide_1'=4,'wide_2'=2,'narrow'=4] {'wide_0'}, use_global_device_ids=true, to_apply=%region_16.17 | all-reduce | flops 1 | bytes 8 | tf_op jit(solution)/shard_map/psum | solution.py:43
  327.1 10.9 %psum.181 = f32[]{:T(128)} all-reduce(f32[]{:T(128)} %psum.180), channel_id=1, replica_groups=mesh['wide_0'=4,'wide_1'=4,'wide_2'=2,'narrow'=4] {'wide_1'}, use_global_device_ids=true, to_apply=%region_17.18 | all-reduce | flops 1 | bytes 8 | tf_op jit(solution)/shard_map/psum | solution.py:43
  341.0 10.3 %psum.183 = f32[]{:T(128)} all-reduce(f32[]{:T(128)} %psum.182), channel_id=1, replica_groups=mesh['wide_0'=4,'wide_1'=4,'wide_2'=2,'narrow'=4] {'narrow'}, use_global_device_ids=true, to_apply=%region_19.20 | all-reduce | flops 1 | bytes 8 | tf_op jit(solution)/shard_map/psum | solution.py:43
  355.1 6.8 %convolution_bitcast_fusion.5 = f32[1,4,128,512]{3,2,1,0:T(8,128)} fusion(f32[4,128,512]{2,1,0:T(8,128)S(1)} %multiply_subtract_fusion.1, s32[512]{0:T(512)S(1)} %multiply_add_fusion.3, f32[512]{0:T(512)S(1)} %fusion.261), kind=kOutput, calls=%fused_computation.37 | convolution fusion | flops 1614544896 | bytes 2101248 | tf_op jit(solution)/shard_map/zyx,kx->zyk/dot_general | solution.py:194
  363.4 21.8 %all_to_all.93 = f32[1,4,128,512]{2,1,0,3:T(4,128)S(1)} all-to-all(f32[1,4,128,512]{2,1,0,3:T(4,128)S(1)} %copy.89), channel_id=1, replica_groups=mesh['wide_0'=4,'wide_1'=4,'wide_2'=2,'narrow'=4] {'wide_0','wide_1','wi..., dimensions={3} | all-to-all | bytes 2097152 | tf_op jit(solution)/shard_map/all_to_all | solution.py:195
  386.9 7.2 %convolution_bitcast_fusion.3 = f32[128,512,4]{0,1,2:T(8,128)S(1)} fusion(f32[128,4,128,4]{2,0,1,3:T(8,128)S(1)} %convolution_bitcast_fusion.4, s32[4,128]{1,0:T(4,128)S(1)} %multiply_add_fusion.4, f32[512]{0:T(512)S(1)} %fusion.261), kind=kOutput, calls=%fused_computation.35 | convolution fusion | flops 1614544896 | bytes 2101248 | tf_op jit(solution)/shard_map/mnyk,lny->mlk/dot_general | solution.py:200
  394.2 6.0 %convolution_bitcast_fusion.2 = f32[128,4,128,4,1]{0,2,3,1,4:T(8,128)S(1)} fusion(f32[128,512,4]{0,1,2:T(8,128)S(1)} %convolution_bitcast_fusion.3, f32[4]{0:T(128)S(1)} %multiply_multiply_fusion.1, f32[128,512]{0,1:T(8,128)S(1)} %broadcast_add_fusion, s32[4,128]{1,0:T(4,128)S(1)} %multiply_add_fusion.4, f32[512]{0:T(512)S(1)} %fusion.261), kind=kOutput, calls=%fused_computation.34 | convolution fusion | flops 1615331328 | bytes 2363408 | tf_op jit(solution)/shard_map/mlk,lny->mnyk/dot_general | solution.py:202
  403.0 23.1 %all_to_all.94 = f32[128,4,128,4]{2,3,1,0:T(4,128)S(1)} all-to-all(f32[128,4,128,4]{2,3,1,0:T(4,128)S(1)} %copy.98), channel_id=1, replica_groups=mesh['wide_0'=4,'wide_1'=4,'wide_2'=2,'narrow'=4] {'wide_0','wide_1','wi..., dimensions={0} | all-to-all | bytes 2097152 | tf_op jit(solution)/shard_map/all_to_all | solution.py:205
  426.2 7.5 %multiply_reduce_fusion.1 = (f32[]{:T(128)}, f32[4,128,512]{2,1,0:T(8,128)}) fusion(f32[4,128,512]{2,1,0:T(8,128)S(1)} %copy-done.21, f32[4,128,512]{1,2,0:T(8,128)S(1)} %bitcast.219, s32[512]{0:T(512)S(1)} %multiply_add_fusion.3, f32[512]{0:T(512)S(1)} %fusion.261), kind=kOutput, calls=%fused_computation.214 | convolution fusion | flops 1615069184 | bytes 3149828 | tf_op jit(solution)/shard_map/zyk,kx->zyx/dot_general | solution.py:206
  433.7 9.5 %psum.184 = f32[]{:T(128)} all-reduce(f32[]{:T(128)} %get-tuple-element.53), channel_id=1, replica_groups=mesh['wide_0'=4,'wide_1'=4,'wide_2'=2,'narrow'=4] {'wide_0'}, use_global_device_ids=true, to_apply=%region_21.22 | all-reduce | flops 1 | bytes 8 | tf_op jit(solution)/shard_map/psum | solution.py:43
  443.2 9.6 %psum.185 = f32[]{:T(128)} all-reduce(f32[]{:T(128)} %psum.184), channel_id=1, replica_groups=mesh['wide_0'=4,'wide_1'=4,'wide_2'=2,'narrow'=4] {'wide_1'}, use_global_device_ids=true, to_apply=%region_22.23 | all-reduce | flops 1 | bytes 8 | tf_op jit(solution)/shard_map/psum | solution.py:43
  452.8 3.1 psum.186
  456.0 9.8 %psum.187 = f32[]{:T(128)} all-reduce(f32[]{:T(128)} %psum.186), channel_id=1, replica_groups=mesh['wide_0'=4,'wide_1'=4,'wide_2'=2,'narrow'=4] {'narrow'}, use_global_device_ids=true, to_apply=%region_24.25 | all-reduce | flops 1 | bytes 8 | tf_op jit(solution)/shard_map/psum | solution.py:43
  470.9 3.6 collective-permute-start.12
  476.9 3.5 collective-permute-start.14
  486.4 9.3 %psum.188 = f32[]{:T(128)} all-reduce(f32[]{:T(128)} %get-tuple-element.13), channel_id=1, replica_groups=mesh['wide_0'=4,'wide_1'=4,'wide_2'=2,'narrow'=4] {'wide_0'}, use_global_device_ids=true, to_apply=%region_26.27 | all-reduce | flops 1 | bytes 8 | tf_op jit(solution)/shard_map/psum | solution.py:43
  495.6 10.9 %psum.189 = f32[]{:T(128)} all-reduce(f32[]{:T(128)} %psum.188), channel_id=1, replica_groups=mesh['wide_0'=4,'wide_1'=4,'wide_2'=2,'narrow'=4] {'wide_1'}, use_global_device_ids=true, to_apply=%region_27.28 | all-reduce | flops 1 | bytes 8 | tf_op jit(solution)/shard_map/psum | solution.py:43
  509.6 10.3 %psum.191 = f32[]{:T(128)} all-reduce(f32[]{:T(128)} %psum.190), channel_id=1, replica_groups=mesh['wide_0'=4,'wide_1'=4,'wide_2'=2,'narrow'=4] {'narrow'}, use_global_device_ids=true, to_apply=%region_29.30 | all-reduce | flops 1 | bytes 8 | tf_op jit(solution)/shard_map/psum | solution.py:43
  521.1 3.5 multiply_subtract_fusion
  (151 shorter events, 88.1 us)
Async XLA Ops:
  0.6 37.9 %copy-start = (f32[128,128]{1,0:T(8,128)S(1)}, f32[128,128]{1,0:T(8,128)}, u32[]{:S(2)}) copy-start(f32[128,128]{1,0:T(8,128)} %param.9) | copy-start | bytes 196612
  0.6 1.6 copy-start.4
  2.2 12.5 %copy-start.23 = (s32[1,1,16]{2,1,0:T(1,128)S(1)}, s32[1,1,16]{2,1,0:T(1,128)}, u32[]{:S(2)}) copy-start(s32[1,1,16]{2,1,0:T(1,128)} %param.7) | copy-start | bytes 196
  2.3 12.8 %collective-permute-start = (f32[2,4,1,512]{3,2,1,0:T(1,128)S(1)}, f32[2,4,1,512]{3,2,1,0:T(1,128)S(1)}, u32[]{:S(2)}, u32[]{:S(2)}) collective-permute-start(f32[2,4,1,512]{3,2,1,0:T(1,128)S(1)} %get-tuple-element.30), channel_id=1, source_target_pairs={{0,1},{1,2},{2,3},{4,5},{5,6},{6,7},{8,9},{9,10},{10,11},{12,13},{... | collective-permute-start | bytes 49160 | tf_op jit(solution)/shard_map/ppermute | solution.py:29
  5.7 9.4 %collective-permute-start.3 = (f32[2,4,1,512]{3,2,1,0:T(1,128)S(1)}, f32[2,4,1,512]{3,2,1,0:T(1,128)S(1)}, u32[]{:S(2)}, u32[]{:S(2)}) collective-permute-start(f32[2,4,1,512]{3,2,1,0:T(1,128)S(1)} %get-tuple-element.31), channel_id=1, source_target_pairs={{1,0},{2,1},{3,2},{5,4},{6,5},{7,6},{9,8},{10,9},{11,10},{13,12},{... | collective-permute-start | bytes 49160 | tf_op jit(solution)/shard_map/ppermute | solution.py:30
  9.2 10.8 %collective-permute-start.1 = (f32[2,1,128,512]{3,2,1,0:T(8,128)}, f32[2,1,128,512]{3,2,1,0:T(8,128)}, u32[]{:S(2)}, u32[]{:S(2)}) collective-permute-start(f32[2,1,128,512]{3,2,1,0:T(8,128)} %get-tuple-element.28), channel_id=1, source_target_pairs={{0,4},{4,8},{8,12},{12,16},{16,20},{20,24},{24,28},{28,32},{32,36}... | collective-permute-start | bytes 1572872 | tf_op jit(solution)/shard_map/ppermute | solution.py:29
  11.1 10.6 %collective-permute-start.2 = (f32[2,1,128,512]{3,2,1,0:T(8,128)}, f32[2,1,128,512]{3,2,1,0:T(8,128)}, u32[]{:S(2)}, u32[]{:S(2)}) collective-permute-start(f32[2,1,128,512]{3,2,1,0:T(8,128)} %get-tuple-element.29), channel_id=1, source_target_pairs={{4,0},{8,4},{12,8},{16,12},{20,16},{24,20},{28,24},{32,28},{36,32}... | collective-permute-start | bytes 1572872 | tf_op jit(solution)/shard_map/ppermute | solution.py:30
  23.6 1.7 copy-start.2
  36.0 3.2 copy-start.22
  44.3 7.0 %copy-start.17 = (f32[4,128,512]{2,1,0:T(8,128)}, f32[4,128,512]{2,1,0:T(8,128)S(1)}, u32[]{:S(2)}) copy-start(f32[4,128,512]{2,1,0:T(8,128)S(1)} %reshape.309) | copy-start | bytes 3145732
  53.9 29.9 %all-to-all-start = ((f32[1,4,128,512]{2,1,0,3:T(4,128)}), f32[1,4,128,512]{2,1,0,3:T(4,128)S(1)}, u32[]{:S(2)}, u32[]{:S(2)}) async-start(f32[1,4,128,512]{2,1,0,3:T(4,128)} %copy.65), calls=%async_computation | async-start | bytes 2097152 | tf_op jit(solution)/shard_map/all_to_all | solution.py:195
  125.0 17.4 %copy-start.3 = (f32[2,6,130,512]{3,2,1,0:T(8,128)S(1)}, f32[2,6,130,512]{3,2,1,0:T(8,128)}, u32[]{:S(2)}) copy-start(f32[2,6,130,512]{3,2,1,0:T(8,128)} %copy-done.2) | copy-start | bytes 9584644
  130.9 13.3 %collective-permute-start.5 = (f32[1,128,512]{2,1,0:T(8,128)S(1)}, f32[1,128,512]{2,1,0:T(8,128)S(1)}, u32[]{:S(2)}, u32[]{:S(2)}) collective-permute-start(f32[1,128,512]{2,1,0:T(8,128)S(1)} %get-tuple-element.47), channel_id=1, source_target_pairs={{0,4},{4,8},{8,12},{12,16},{16,20},{20,24},{24,28},{28,32},{32,36}... | collective-permute-start | bytes 786440 | tf_op jit(solution)/shard_map/ppermute | solution.py:29
  132.8 11.4 %collective-permute-start.4 = (f32[1,128,512]{2,1,0:T(8,128)S(1)}, f32[1,128,512]{2,1,0:T(8,128)S(1)}, u32[]{:S(2)}, u32[]{:S(2)}) collective-permute-start(f32[1,128,512]{2,1,0:T(8,128)S(1)} %get-tuple-element.48), channel_id=1, source_target_pairs={{4,0},{8,4},{12,8},{16,12},{20,16},{24,20},{28,24},{32,28},{36,32}... | collective-permute-start | bytes 786440 | tf_op jit(solution)/shard_map/ppermute | solution.py:30
  136.5 6.5 %collective-permute-start.7 = (f32[4,1,512]{2,1,0:T(1,128)S(1)}, f32[4,1,512]{2,1,0:T(1,128)S(1)}, u32[]{:S(2)}, u32[]{:S(2)}) collective-permute-start(f32[4,1,512]{2,1,0:T(1,128)S(1)} %get-tuple-element.49), channel_id=1, source_target_pairs={{0,1},{1,2},{2,3},{4,5},{5,6},{6,7},{8,9},{9,10},{10,11},{12,13},{... | collective-permute-start | bytes 24584 | tf_op jit(solution)/shard_map/ppermute | solution.py:29
  138.6 5.5 %collective-permute-start.6 = (f32[4,1,512]{2,1,0:T(1,128)S(1)}, f32[4,1,512]{2,1,0:T(1,128)S(1)}, u32[]{:S(2)}, u32[]{:S(2)}) collective-permute-start(f32[4,1,512]{2,1,0:T(1,128)S(1)} %get-tuple-element.50), channel_id=1, source_target_pairs={{1,0},{2,1},{3,2},{5,4},{6,5},{7,6},{9,8},{10,9},{11,10},{13,12},{... | collective-permute-start | bytes 24584 | tf_op jit(solution)/shard_map/ppermute | solution.py:30
  142.9 2.0 copy-start.18
  190.0 71.0 %copy-start.19 = (f32[4,128,512]{2,1,0:T(8,128)}, f32[4,128,512]{2,1,0:T(8,128)S(1)}, u32[]{:S(2)}) copy-start(f32[4,128,512]{2,1,0:T(8,128)S(1)} %multiply_subtract_fusion.2) | copy-start | bytes 3145732
  300.7 14.8 %copy-start.13 = (f32[4,128,512]{2,1,0:T(8,128)S(1)}, f32[4,128,512]{2,1,0:T(8,128)}, u32[]{:S(2)}) copy-start(f32[4,128,512]{2,1,0:T(8,128)} %get-tuple-element.22) | copy-start | bytes 3145732
  300.7 14.8 %copy-start.15 = (f32[4,128,512]{2,1,0:T(8,128)S(1)}, f32[4,128,512]{2,1,0:T(8,128)}, u32[]{:S(2)}) copy-start(f32[4,128,512]{2,1,0:T(8,128)} %get-tuple-element.23) | copy-start | bytes 3145732
  301.0 14.6 %copy-start.11 = (f32[4,128,512]{2,1,0:T(8,128)S(1)}, f32[4,128,512]{2,1,0:T(8,128)}, u32[]{:S(2)}) copy-start(f32[4,128,512]{2,1,0:T(8,128)} %get-tuple-element.21) | copy-start | bytes 3145732
  301.0 14.6 %copy-start.5 = (f32[4,128,512]{2,1,0:T(8,128)S(1)}, f32[4,128,512]{2,1,0:T(8,128)}, u32[]{:S(2)}) copy-start(f32[4,128,512]{2,1,0:T(8,128)} %get-tuple-element.18) | copy-start | bytes 3145732
  301.0 14.6 %copy-start.7 = (f32[4,128,512]{2,1,0:T(8,128)S(1)}, f32[4,128,512]{2,1,0:T(8,128)}, u32[]{:S(2)}) copy-start(f32[4,128,512]{2,1,0:T(8,128)} %get-tuple-element.19) | copy-start | bytes 3145732
  301.0 14.6 %copy-start.9 = (f32[4,128,512]{2,1,0:T(8,128)S(1)}, f32[4,128,512]{2,1,0:T(8,128)}, u32[]{:S(2)}) copy-start(f32[4,128,512]{2,1,0:T(8,128)} %get-tuple-element.20) | copy-start | bytes 3145732
  301.0 13.7 %collective-permute-start.9 = (f32[1,128,512]{2,1,0:T(8,128)S(1)}, f32[1,128,512]{2,1,0:T(8,128)S(1)}, u32[]{:S(2)}, u32[]{:S(2)}) collective-permute-start(f32[1,128,512]{2,1,0:T(8,128)S(1)} %get-tuple-element.43), channel_id=1, source_target_pairs={{0,4},{4,8},{8,12},{12,16},{16,20},{20,24},{24,28},{28,32},{32,36}... | collective-permute-start | bytes 786440 | tf_op jit(solution)/shard_map/ppermute | solution.py:29
  303.2 11.5 %collective-permute-start.8 = (f32[1,128,512]{2,1,0:T(8,128)S(1)}, f32[1,128,512]{2,1,0:T(8,128)S(1)}, u32[]{:S(2)}, u32[]{:S(2)}) collective-permute-start(f32[1,128,512]{2,1,0:T(8,128)S(1)} %get-tuple-element.44), channel_id=1, source_target_pairs={{4,0},{8,4},{12,8},{16,12},{20,16},{24,20},{28,24},{32,28},{36,32}... | collective-permute-start | bytes 786440 | tf_op jit(solution)/shard_map/ppermute | solution.py:30
  306.9 5.9 %collective-permute-start.11 = (f32[4,1,512]{2,1,0:T(1,128)S(1)}, f32[4,1,512]{2,1,0:T(1,128)S(1)}, u32[]{:S(2)}, u32[]{:S(2)}) collective-permute-start(f32[4,1,512]{2,1,0:T(1,128)S(1)} %get-tuple-element.45), channel_id=1, source_target_pairs={{0,1},{1,2},{2,3},{4,5},{5,6},{6,7},{8,9},{9,10},{10,11},{12,13},{... | collective-permute-start | bytes 24584 | tf_op jit(solution)/shard_map/ppermute | solution.py:29
  309.2 5.5 %collective-permute-start.10 = (f32[4,1,512]{2,1,0:T(1,128)S(1)}, f32[4,1,512]{2,1,0:T(1,128)S(1)}, u32[]{:S(2)}, u32[]{:S(2)}) collective-permute-start(f32[4,1,512]{2,1,0:T(1,128)S(1)} %get-tuple-element.46), channel_id=1, source_target_pairs={{1,0},{2,1},{3,2},{5,4},{6,5},{7,6},{9,8},{10,9},{11,10},{13,12},{... | collective-permute-start | bytes 24584 | tf_op jit(solution)/shard_map/ppermute | solution.py:30
  354.1 1.0 copy-start.20
  402.9 23.3 %copy-start.21 = (f32[4,128,512]{2,1,0:T(8,128)S(1)}, f32[4,128,512]{2,1,0:T(8,128)}, u32[]{:S(2)}) copy-start(f32[4,128,512]{2,1,0:T(8,128)} %copy-done.20) | copy-start | bytes 3145732
  467.0 16.2 %copy-start.14 = (f32[4,128,512]{2,1,0:T(8,128)S(1)}, f32[4,128,512]{2,1,0:T(8,128)}, u32[]{:S(2)}) copy-start(f32[4,128,512]{2,1,0:T(8,128)} %get-tuple-element.22) | copy-start | bytes 3145732
  467.0 16.2 %copy-start.16 = (f32[4,128,512]{2,1,0:T(8,128)S(1)}, f32[4,128,512]{2,1,0:T(8,128)}, u32[]{:S(2)}) copy-start(f32[4,128,512]{2,1,0:T(8,128)} %get-tuple-element.23) | copy-start | bytes 3145732
  468.6 14.6 %copy-start.12 = (f32[4,128,512]{2,1,0:T(8,128)S(1)}, f32[4,128,512]{2,1,0:T(8,128)}, u32[]{:S(2)}) copy-start(f32[4,128,512]{2,1,0:T(8,128)} %get-tuple-element.21) | copy-start | bytes 3145732
  468.7 14.6 %copy-start.6 = (f32[4,128,512]{2,1,0:T(8,128)S(1)}, f32[4,128,512]{2,1,0:T(8,128)}, u32[]{:S(2)}) copy-start(f32[4,128,512]{2,1,0:T(8,128)} %get-tuple-element.18) | copy-start | bytes 3145732
  468.7 14.6 %copy-start.8 = (f32[4,128,512]{2,1,0:T(8,128)S(1)}, f32[4,128,512]{2,1,0:T(8,128)}, u32[]{:S(2)}) copy-start(f32[4,128,512]{2,1,0:T(8,128)} %get-tuple-element.19) | copy-start | bytes 3145732
  468.7 14.6 %copy-start.10 = (f32[4,128,512]{2,1,0:T(8,128)S(1)}, f32[4,128,512]{2,1,0:T(8,128)}, u32[]{:S(2)}) copy-start(f32[4,128,512]{2,1,0:T(8,128)} %get-tuple-element.20) | copy-start | bytes 3145732
  468.7 13.7 %collective-permute-start.13 = (f32[1,128,512]{2,1,0:T(8,128)S(1)}, f32[1,128,512]{2,1,0:T(8,128)S(1)}, u32[]{:S(2)}, u32[]{:S(2)}) collective-permute-start(f32[1,128,512]{2,1,0:T(8,128)S(1)} %get-tuple-element.39), channel_id=1, source_target_pairs={{0,4},{4,8},{8,12},{12,16},{16,20},{20,24},{24,28},{28,32},{32,36}... | collective-permute-start | bytes 786440 | tf_op jit(solution)/shard_map/ppermute | solution.py:29
  470.9 11.5 %collective-permute-start.12 = (f32[1,128,512]{2,1,0:T(8,128)S(1)}, f32[1,128,512]{2,1,0:T(8,128)S(1)}, u32[]{:S(2)}, u32[]{:S(2)}) collective-permute-start(f32[1,128,512]{2,1,0:T(8,128)S(1)} %get-tuple-element.40), channel_id=1, source_target_pairs={{4,0},{8,4},{12,8},{16,12},{20,16},{24,20},{28,24},{32,28},{36,32}... | collective-permute-start | bytes 786440 | tf_op jit(solution)/shard_map/ppermute | solution.py:30
  474.6 5.9 %collective-permute-start.15 = (f32[4,1,512]{2,1,0:T(1,128)S(1)}, f32[4,1,512]{2,1,0:T(1,128)S(1)}, u32[]{:S(2)}, u32[]{:S(2)}) collective-permute-start(f32[4,1,512]{2,1,0:T(1,128)S(1)} %get-tuple-element.41), channel_id=1, source_target_pairs={{0,1},{1,2},{2,3},{4,5},{5,6},{6,7},{8,9},{9,10},{10,11},{12,13},{... | collective-permute-start | bytes 24584 | tf_op jit(solution)/shard_map/ppermute | solution.py:29
  476.9 5.5 %collective-permute-start.14 = (f32[4,1,512]{2,1,0:T(1,128)S(1)}, f32[4,1,512]{2,1,0:T(1,128)S(1)}, u32[]{:S(2)}, u32[]{:S(2)}) collective-permute-start(f32[4,1,512]{2,1,0:T(1,128)S(1)} %get-tuple-element.42), channel_id=1, source_target_pairs={{1,0},{2,1},{3,2},{5,4},{6,5},{7,6},{9,8},{10,9},{11,10},{13,12},{... | collective-permute-start | bytes 24584 | tf_op jit(solution)/shard_map/ppermute | solution.py:30
  521.1 3.5 copy-start.1
where the time goes:
time: 535 us; the launch traced here: 525 us
  blocking collectives  278 us (52%)
  matrix products  92.4 us (17%)
  starting transfers between devices  58.2 us (11%)
  other arithmetic  36.1 us (7%)
  waiting for transfers between devices  29.2 us (5%)
  local copies, waits for them, and re-layouts  22.7 us (4%)
  between operations  8.14 us (2%)
    psum x20, blocking collectives, over_axes(): array = lax.psum(array, axis)  165 us
    all_to_all x3, blocking collectives, precondition(): lax.all_to_all(planes, WIDE_NARROW, split_axis=0, concat_axis=3, tiled=True)  69 us
    all_to_all x2, blocking collectives, precondition(): lax.all_to_all(spectrum[None], WIDE_NARROW, split_axis=3, concat_axis=0,...  43.6 us
    ppermute x8, starting transfers between devices, padded_2(): lax.ppermute(initial, axis, [(b, a) for a, b in up])  27.8 us
    dot_general x3, matrix products, precondition(): planes = jnp.einsum('mnyk,lny->mlk', planes, table_y, precision=highest)  21.7 us
    dot_general x3, matrix products, precondition(): spectrum = jnp.einsum('zyx,kx->zyk', remainder, table_x, precision=highest)  20.5 us
    dot_general x3, matrix products, precondition(): return jnp.einsum('zyk,kx->zyx', slabs[0], table_x, precision=highest)  19.9 us
    dot_general x3, matrix products, precondition(): jnp.einsum('mlk,lny->mnyk', planes / denom, table_y, precision=highest)  18.4 us
  transfers between devices with their start and end apart: 17, of which 6 were waited for; matrix products, arithmetic and copies ran while one was open for 0% of the time, Pallas kernels for 0%

commit v1 on v0

--- a/solution.py
+++ b/solution.py
@@ -40,7 +40,7 @@
 
 def over_axes(array, axes):
     for axis in axes:
-        array = lax.psum(array, axis)
+        array = jnp.sum(lax.all_gather(array, axis), axis=0)
     return array
 
 

time: 535 us -> 569 us (1.064)
  the two profiles are of different devices: /device:TPU:34 before, /device:TPU:0 now
where the time goes in v1:
time: 569 us; the launch traced here: 558 us
  blocking collectives  240 us (42%)
  matrix products  92.6 us (16%)
  starting transfers between devices  65.9 us (12%)
  local copies, waits for them, and re-layouts  58.8 us (10%)
  other arithmetic  51.2 us (9%)
  waiting for transfers between devices  40.9 us (7%)
  between operations  8.53 us (1%)
    unnamed x20, blocking collectives  149 us
    all_to_all x2, blocking collectives, precondition(): lax.all_to_all(planes, WIDE_NARROW, split_axis=0, concat_axis=3, tiled=True)  46.1 us
    all_to_all x2, blocking collectives, precondition(): lax.all_to_all(spectrum[None], WIDE_NARROW, split_axis=3, concat_axis=0,...  45.8 us
    unnamed x111, local copies, waits for them, and re-layouts  38.7 us
    ppermute x8, starting transfers between devices, padded_2(): lax.ppermute(last, axis, up)  31.2 us
    dot_general x3, matrix products, precondition(): planes = jnp.einsum('mnyk,lny->mlk', planes, table_y, precision=highest)  21.7 us
    dot_general x3, matrix products, precondition(): spectrum = jnp.einsum('zyx,kx->zyk', remainder, table_x, precision=highest)  20.5 us
    dot_general x3, matrix products, precondition(): return jnp.einsum('zyk,kx->zyx', slabs[0], table_x, precision=highest)  19.9 us
  transfers between devices with their start and end apart: 18, of which 6 were waited for; matrix products, arithmetic and copies ran while one was open for 1% of the time, Pallas kernels for 0%

profile of v1, /device:TPU:0, one launch (start us, length us, event | category | flops | bytes accessed | tf_op | source)
XLA Modules:
  0.0 558.4 jit_solution(16336040777913412727)
XLA Ops:
  3.6 4.5 collective-permute-start
  10.5 3.9 collective-permute-start.1
  20.9 4.9 fusion.6
  38.0 7.0 %convolution_bitcast_fusion.15 = f32[1,4,128,512]{3,2,1,0:T(8,128)} fusion(f32[4,128,512]{2,1,0:T(8,128)S(1)} %reshape.309, s32[512]{0:T(512)S(1)} %multiply_add_fusion.3, f32[512]{0:T(512)S(1)} %fusion.261), kind=kOutput, calls=%fused_computation.47 | convolution fusion | flops 1614544896 | bytes 2101248 | tf_op jit(solution)/shard_map/zyx,kx->zyk/dot_general | solution.py:194
  47.5 19.2 %all-to-all-start = ((f32[1,4,128,512]{2,1,0,3:T(4,128)}), f32[1,4,128,512]{2,1,0,3:T(4,128)S(1)}, u32[]{:S(2)}, u32[]{:S(2)}) async-start(f32[1,4,128,512]{2,1,0,3:T(4,128)} %copy.65), calls=%async_computation | async-start | bytes 2097152 | tf_op jit(solution)/shard_map/all_to_all | solution.py:195
  67.1 18.6 %all-to-all-done = f32[1,4,128,512]{2,1,0,3:T(4,128)S(1)} async-done(((f32[1,4,128,512]{2,1,0,3:T(4,128)}), f32[1,4,128,512]{2,1,0,3:T(4,128)S(1)}, u32[]{:S(2)}, u32[]{:S(2)}) %all-to-all-start) | async-done | bytes 1048608 | tf_op jit(solution)/shard_map/all_to_all | solution.py:195
  87.3 7.2 %convolution_bitcast_fusion.13 = f32[128,512,4]{0,1,2:T(8,128)S(1)} fusion(f32[128,4,128,4]{2,0,1,3:T(8,128)S(1)} %convolution_bitcast_fusion.14, s32[4,128]{1,0:T(4,128)S(1)} %multiply_add_fusion.4, f32[512]{0:T(512)S(1)} %fusion.261), kind=kOutput, calls=%fused_computation.45 | convolution fusion | flops 1614544896 | bytes 2101248 | tf_op jit(solution)/shard_map/mnyk,lny->mlk/dot_general | solution.py:200
  94.6 6.3 %convolution_bitcast_fusion.12 = f32[128,4,128,4,1]{0,2,3,1,4:T(8,128)S(1)} fusion(f32[128,512,4]{0,1,2:T(8,128)S(1)} %convolution_bitcast_fusion.13, f32[4]{0:T(128)S(1)} %multiply_multiply_fusion.1, f32[128,512]{0,1:T(8,128)S(1)} %broadcast_add_fusion, s32[4,128]{1,0:T(4,128)S(1)} %multiply_add_fusion.4, f32[512]{0:T(512)S(1)} %fusion.261), kind=kOutput, calls=%fused_computation.44 | convolution fusion | flops 1615331328 | bytes 2363408 | tf_op jit(solution)/shard_map/mlk,lny->mnyk/dot_general | solution.py:202
  104.6 4.6 all-to-all-start.1
  109.8 18.3 %all-to-all-done.1 = f32[128,4,128,4]{2,3,1,0:T(4,128)S(1)} async-done(((f32[128,4,128,4]{2,3,1,0:T(4,128)}), f32[128,4,128,4]{2,3,1,0:T(4,128)S(1)}, u32[]{:S(2)}, u32[]{:S(2)}) %all-to-all-start.1) | async-done | bytes 1048608 | tf_op jit(solution)/shard_map/all_to_all | solution.py:205
  128.3 5.8 %fusion.126 = f32[4,128,512]{2,1,0:T(8,128)S(1)} fusion(f32[4,128,512]{1,2,0:T(8,128)S(1)} %bitcast.249, s32[512]{0:T(512)S(1)} %multiply_add_fusion.3, f32[512]{0:T(512)S(1)} %fusion.261), kind=kOutput, calls=%fused_computation.235 | convolution fusion | flops 1614544896 | bytes 2101248 | tf_op jit(solution)/shard_map/zyk,kx->zyx/dot_general | solution.py:206
  135.5 3.0 collective-permute-start.5
  139.9 4.5 collective-permute-start.7
  146.6 7.6 %multiply_reduce_fusion.4 = (f32[]{:T(128)}, f32[]{:T(128)}, f32[4,128,512]{2,1,0:T(8,128)}, f32[4,128,512]{2,1,0:T(8,128)}, f32[4,128,512]{2,1,0:T(8,128)}, /*i...) fusion(f32[4,128,512]{2,1,0:T(8,128)S(1)} %fusion.126, ...), kind=kLoop, calls=%fused_computation.222 | loop fusion | flops 12845054 | bytes 25714696 | tf_op jit(solution)/shard_map/reduce_sum | solution.py:216
  157.5 9.7 %all-reduce.38 = (f32[4]{0:T(128)S(1)}, f32[4]{0:T(128)S(1)}) all-reduce(f32[4]{0:T(128)S(1)} %dynamic-update-slice, f32[4]{0:T(128)S(1)} %dynamic-update-slice.4), channel_id=1, replica_groups=mesh['wide_0'=4,'wide_1'=4,'wide_2'=2,'narrow'=4] {'wide_0'}, use_global_device_ids=true, to_apply=%add.12 | all-reduce | flops 8 | bytes 64
  171.8 8.2 %all-reduce.37 = (f32[4]{0:T(128)S(1)}, f32[4]{0:T(128)S(1)}) all-reduce(f32[4]{0:T(128)S(1)} %dynamic-update-slice.1, f32[4]{0:T(128)S(1)} %dynamic-update-slice.5), channel_id=1, replica_groups=mesh['wide_0'=4,'wide_1'=4,'wide_2'=2,'narrow'=4] {'wide_1'}, use_global_device_ids=true, to_apply=%add.13 | all-reduce | flops 8 | bytes 64
  184.6 2.6 all-reduce.39
  191.2 10.0 %all-reduce.36 = (f32[4]{0:T(128)S(1)}, f32[4]{0:T(128)S(1)}) all-reduce(f32[4]{0:T(128)S(1)} %dynamic-update-slice.3, f32[4]{0:T(128)S(1)} %dynamic-update-slice.7), channel_id=1, replica_groups=mesh['wide_0'=4,'wide_1'=4,'wide_2'=2,'narrow'=4] {'narrow'}, use_global_device_ids=true, to_apply=%add.15 | all-reduce | flops 8 | bytes 64
  205.6 6.8 %convolution_bitcast_fusion.10 = f32[1,4,128,512]{3,2,1,0:T(8,128)} fusion(f32[4,128,512]{2,1,0:T(8,128)S(1)} %multiply_subtract_fusion.2, s32[512]{0:T(512)S(1)} %multiply_add_fusion.3, f32[512]{0:T(512)S(1)} %fusion.261), kind=kOutput, calls=%fused_computation.42 | convolution fusion | flops 1614544896 | bytes 2101248 | tf_op jit(solution)/shard_map/zyx,kx->zyk/dot_general | solution.py:194
  214.0 22.9 %all_to_all.90 = f32[1,4,128,512]{2,1,0,3:T(4,128)S(1)} all-to-all(f32[1,4,128,512]{2,1,0,3:T(4,128)S(1)} %copy.77), channel_id=1, replica_groups=mesh['wide_0'=4,'wide_1'=4,'wide_2'=2,'narrow'=4] {'wide_0','wide_1','wi..., dimensions={3} | all-to-all | bytes 2097152 | tf_op jit(solution)/shard_map/all_to_all | solution.py:195
  238.5 7.2 %convolution_bitcast_fusion.8 = f32[128,512,4]{0,1,2:T(8,128)S(1)} fusion(f32[128,4,128,4]{2,0,1,3:T(8,128)S(1)} %convolution_bitcast_fusion.9, s32[4,128]{1,0:T(4,128)S(1)} %multiply_add_fusion.4, f32[512]{0:T(512)S(1)} %fusion.261), kind=kOutput, calls=%fused_computation.40 | convolution fusion | flops 1614544896 | bytes 2101248 | tf_op jit(solution)/shard_map/mnyk,lny->mlk/dot_general | solution.py:200
  245.8 6.3 %convolution_bitcast_fusion.7 = f32[128,4,128,4,1]{0,2,3,1,4:T(8,128)S(1)} fusion(f32[128,512,4]{0,1,2:T(8,128)S(1)} %convolution_bitcast_fusion.8, f32[4]{0:T(128)S(1)} %multiply_multiply_fusion.1, f32[128,512]{0,1:T(8,128)S(1)} %broadcast_add_fusion, s32[4,128]{1,0:T(4,128)S(1)} %multiply_add_fusion.4, f32[512]{0:T(512)S(1)} %fusion.261), kind=kOutput, calls=%fused_computation.39 | convolution fusion | flops 1615331328 | bytes 2363408 | tf_op jit(solution)/shard_map/mlk,lny->mnyk/dot_general | solution.py:202
  254.8 23.1 %all_to_all.91 = f32[128,4,128,4]{2,3,1,0:T(4,128)S(1)} all-to-all(f32[128,4,128,4]{2,3,1,0:T(4,128)S(1)} %copy.86), channel_id=1, replica_groups=mesh['wide_0'=4,'wide_1'=4,'wide_2'=2,'narrow'=4] {'wide_0','wide_1','wi..., dimensions={0} | all-to-all | bytes 2097152 | tf_op jit(solution)/shard_map/all_to_all | solution.py:205
  278.1 6.6 %multiply_reduce_fusion.3 = (f32[]{:T(128)}, f32[4,128,512]{2,1,0:T(8,128)S(1)}) fusion(f32[4,128,512]{2,1,0:T(8,128)S(1)} %multiply_subtract_fusion.2, f32[4,128,512]{1,2,0:T(8,128)S(1)} %bitcast.248, s32[512]{0:T(512)S(1)} %multiply_add_fusion.3, f32[512]{0:T(512)S(1)} %fusion.261), kind=kOutput, calls=%fused_computation.219 | convolution fusion | flops 1615069184 | bytes 3149828 | tf_op jit(solution)/shard_map/zyk,kx->zyx/dot_general | solution.py:206
  286.0 8.8 %all-reduce.20 = f32[4]{0:T(128)S(1)} all-reduce(f32[4]{0:T(128)S(1)} %dynamic-update-slice.8), channel_id=1, replica_groups=mesh['wide_0'=4,'wide_1'=4,'wide_2'=2,'narrow'=4] {'wide_0'}, use_global_device_ids=true, to_apply=%add.20 | all-reduce | flops 4 | bytes 32
  296.8 8.5 %all-reduce.21 = f32[4]{0:T(128)S(1)} all-reduce(f32[4]{0:T(128)S(1)} %dynamic-update-slice.9), channel_id=1, replica_groups=mesh['wide_0'=4,'wide_1'=4,'wide_2'=2,'narrow'=4] {'wide_1'}, use_global_device_ids=true, to_apply=%add.21 | all-reduce | flops 4 | bytes 32
  311.7 8.5 %all-reduce.23 = f32[4]{0:T(128)S(1)} all-reduce(f32[4]{0:T(128)S(1)} %dynamic-update-slice.11), channel_id=1, replica_groups=mesh['wide_0'=4,'wide_1'=4,'wide_2'=2,'narrow'=4] {'narrow'}, use_global_device_ids=true, to_apply=%add.23 | all-reduce | flops 4 | bytes 32
  324.1 3.0 collective-permute-start.9
  328.5 4.5 collective-permute-start.11
  338.8 9.1 %all-reduce.24 = f32[4]{0:T(128)S(1)} all-reduce(f32[4]{0:T(128)S(1)} %dynamic-update-slice.12), channel_id=1, replica_groups=mesh['wide_0'=4,'wide_1'=4,'wide_2'=2,'narrow'=4] {'wide_0'}, use_global_device_ids=true, to_apply=%add.24 | all-reduce | flops 4 | bytes 32
  349.9 9.2 %all-reduce.25 = f32[4]{0:T(128)S(1)} all-reduce(f32[4]{0:T(128)S(1)} %dynamic-update-slice.13), channel_id=1, replica_groups=mesh['wide_0'=4,'wide_1'=4,'wide_2'=2,'narrow'=4] {'wide_1'}, use_global_device_ids=true, to_apply=%add.25 | all-reduce | flops 4 | bytes 32
  365.5 10.0 %all-reduce.27 = f32[4]{0:T(128)S(1)} all-reduce(f32[4]{0:T(128)S(1)} %dynamic-update-slice.15), channel_id=1, replica_groups=mesh['wide_0'=4,'wide_1'=4,'wide_2'=2,'narrow'=4] {'narrow'}, use_global_device_ids=true, to_apply=%add.27 | all-reduce | flops 4 | bytes 32
  379.9 6.8 %convolution_bitcast_fusion.5 = f32[1,4,128,512]{3,2,1,0:T(8,128)} fusion(f32[4,128,512]{2,1,0:T(8,128)S(1)} %multiply_subtract_fusion.1, s32[512]{0:T(512)S(1)} %multiply_add_fusion.3, f32[512]{0:T(512)S(1)} %fusion.261), kind=kOutput, calls=%fused_computation.37 | convolution fusion | flops 1614544896 | bytes 2101248 | tf_op jit(solution)/shard_map/zyx,kx->zyk/dot_general | solution.py:194
  388.3 22.9 %all_to_all.92 = f32[1,4,128,512]{2,1,0,3:T(4,128)S(1)} all-to-all(f32[1,4,128,512]{2,1,0,3:T(4,128)S(1)} %copy.89), channel_id=1, replica_groups=mesh['wide_0'=4,'wide_1'=4,'wide_2'=2,'narrow'=4] {'wide_0','wide_1','wi..., dimensions={3} | all-to-all | bytes 2097152 | tf_op jit(solution)/shard_map/all_to_all | solution.py:195
  412.9 7.2 %convolution_bitcast_fusion.3 = f32[128,512,4]{0,1,2:T(8,128)S(1)} fusion(f32[128,4,128,4]{2,0,1,3:T(8,128)S(1)} %convolution_bitcast_fusion.4, s32[4,128]{1,0:T(4,128)S(1)} %multiply_add_fusion.4, f32[512]{0:T(512)S(1)} %fusion.261), kind=kOutput, calls=%fused_computation.35 | convolution fusion | flops 1614544896 | bytes 2101248 | tf_op jit(solution)/shard_map/mnyk,lny->mlk/dot_general | solution.py:200
  420.1 6.0 %convolution_bitcast_fusion.2 = f32[128,4,128,4,1]{0,2,3,1,4:T(8,128)S(1)} fusion(f32[128,512,4]{0,1,2:T(8,128)S(1)} %convolution_bitcast_fusion.3, f32[4]{0:T(128)S(1)} %multiply_multiply_fusion.1, f32[128,512]{0,1:T(8,128)S(1)} %broadcast_add_fusion, s32[4,128]{1,0:T(4,128)S(1)} %multiply_add_fusion.4, f32[512]{0:T(512)S(1)} %fusion.261), kind=kOutput, calls=%fused_computation.34 | convolution fusion | flops 1615331328 | bytes 2363408 | tf_op jit(solution)/shard_map/mlk,lny->mnyk/dot_general | solution.py:202
  428.9 23.0 %all_to_all.93 = f32[128,4,128,4]{2,3,1,0:T(4,128)S(1)} all-to-all(f32[128,4,128,4]{2,3,1,0:T(4,128)S(1)} %copy.98), channel_id=1, replica_groups=mesh['wide_0'=4,'wide_1'=4,'wide_2'=2,'narrow'=4] {'wide_0','wide_1','wi..., dimensions={0} | all-to-all | bytes 2097152 | tf_op jit(solution)/shard_map/all_to_all | solution.py:205
  452.2 7.5 %multiply_reduce_fusion.1 = (f32[]{:T(128)}, f32[4,128,512]{2,1,0:T(8,128)}) fusion(f32[4,128,512]{2,1,0:T(8,128)S(1)} %copy-done.21, f32[4,128,512]{1,2,0:T(8,128)S(1)} %bitcast.247, s32[512]{0:T(512)S(1)} %multiply_add_fusion.3, f32[512]{0:T(512)S(1)} %fusion.261), kind=kOutput, calls=%fused_computation.214 | convolution fusion | flops 1615069184 | bytes 3149828 | tf_op jit(solution)/shard_map/zyk,kx->zyx/dot_general | solution.py:206
  460.9 8.8 %all-reduce.28 = f32[4]{0:T(128)S(1)} all-reduce(f32[4]{0:T(128)S(1)} %dynamic-update-slice.16), channel_id=1, replica_groups=mesh['wide_0'=4,'wide_1'=4,'wide_2'=2,'narrow'=4] {'wide_0'}, use_global_device_ids=true, to_apply=%add.28 | all-reduce | flops 4 | bytes 32
  471.6 8.5 %all-reduce.29 = f32[4]{0:T(128)S(1)} all-reduce(f32[4]{0:T(128)S(1)} %dynamic-update-slice.17), channel_id=1, replica_groups=mesh['wide_0'=4,'wide_1'=4,'wide_2'=2,'narrow'=4] {'wide_1'}, use_global_device_ids=true, to_apply=%add.29 | all-reduce | flops 4 | bytes 32
  486.4 8.5 %all-reduce.31 = f32[4]{0:T(128)S(1)} all-reduce(f32[4]{0:T(128)S(1)} %dynamic-update-slice.19), channel_id=1, replica_groups=mesh['wide_0'=4,'wide_1'=4,'wide_2'=2,'narrow'=4] {'narrow'}, use_global_device_ids=true, to_apply=%add.31 | all-reduce | flops 4 | bytes 32
  500.1 3.0 collective-permute-start.13
  504.4 4.5 collective-permute-start.15
  511.2 3.1 multiply_reduce_fusion
  515.6 9.1 %all-reduce.32 = f32[4]{0:T(128)S(1)} all-reduce(f32[4]{0:T(128)S(1)} %dynamic-update-slice.20), channel_id=1, replica_groups=mesh['wide_0'=4,'wide_1'=4,'wide_2'=2,'narrow'=4] {'wide_0'}, use_global_device_ids=true, to_apply=%add.32 | all-reduce | flops 4 | bytes 32
  526.8 9.2 %all-reduce.33 = f32[4]{0:T(128)S(1)} all-reduce(f32[4]{0:T(128)S(1)} %dynamic-update-slice.21), channel_id=1, replica_groups=mesh['wide_0'=4,'wide_1'=4,'wide_2'=2,'narrow'=4] {'wide_1'}, use_global_device_ids=true, to_apply=%add.33 | all-reduce | flops 4 | bytes 32
  542.7 10.0 %all-reduce.35 = f32[4]{0:T(128)S(1)} all-reduce(f32[4]{0:T(128)S(1)} %dynamic-update-slice.23), channel_id=1, replica_groups=mesh['wide_0'=4,'wide_1'=4,'wide_2'=2,'narrow'=4] {'narrow'}, use_global_device_ids=true, to_apply=%add.35 | all-reduce | flops 4 | bytes 32
  554.7 3.5 multiply_subtract_fusion
  (236 shorter events, 127.4 us)
Async XLA Ops:
  0.6 31.5 %copy-start = (f32[128,128]{1,0:T(8,128)S(1)}, f32[128,128]{1,0:T(8,128)}, u32[]{:S(2)}) copy-start(f32[128,128]{1,0:T(8,128)} %param.9) | copy-start | bytes 196612
  0.6 1.6 copy-start.4
  2.2 12.1 %copy-start.23 = (s32[1,1,16]{2,1,0:T(1,128)S(1)}, s32[1,1,16]{2,1,0:T(1,128)}, u32[]{:S(2)}) copy-start(s32[1,1,16]{2,1,0:T(1,128)} %param.7) | copy-start | bytes 196
  2.3 12.4 %collective-permute-start.3 = (f32[2,4,1,512]{3,2,1,0:T(1,128)S(1)}, f32[2,4,1,512]{3,2,1,0:T(1,128)S(1)}, u32[]{:S(2)}, u32[]{:S(2)}) collective-permute-start(f32[2,4,1,512]{3,2,1,0:T(1,128)S(1)} %get-tuple-element.31), channel_id=1, source_target_pairs={{1,0},{2,1},{3,2},{5,4},{6,5},{7,6},{9,8},{10,9},{11,10},{13,12},{... | collective-permute-start | bytes 49160 | tf_op jit(solution)/shard_map/ppermute | solution.py:30
  3.6 11.1 %collective-permute-start = (f32[2,4,1,512]{3,2,1,0:T(1,128)S(1)}, f32[2,4,1,512]{3,2,1,0:T(1,128)S(1)}, u32[]{:S(2)}, u32[]{:S(2)}) collective-permute-start(f32[2,4,1,512]{3,2,1,0:T(1,128)S(1)} %get-tuple-element.30), channel_id=1, source_target_pairs={{0,1},{1,2},{2,3},{4,5},{5,6},{6,7},{8,9},{9,10},{10,11},{12,13},{... | collective-permute-start | bytes 49160 | tf_op jit(solution)/shard_map/ppermute | solution.py:29
  9.2 5.5 collective-permute-start.2
  10.5 4.9 collective-permute-start.1
  17.2 1.7 copy-start.2
  29.6 3.2 copy-start.22
  38.0 7.0 %copy-start.17 = (f32[4,128,512]{2,1,0:T(8,128)}, f32[4,128,512]{2,1,0:T(8,128)S(1)}, u32[]{:S(2)}) copy-start(f32[4,128,512]{2,1,0:T(8,128)S(1)} %reshape.309) | copy-start | bytes 3145732
  47.5 38.1 %all-to-all-start = ((f32[1,4,128,512]{2,1,0,3:T(4,128)}), f32[1,4,128,512]{2,1,0,3:T(4,128)S(1)}, u32[]{:S(2)}, u32[]{:S(2)}) async-start(f32[1,4,128,512]{2,1,0,3:T(4,128)} %copy.65), calls=%async_computation | async-start | bytes 2097152 | tf_op jit(solution)/shard_map/all_to_all | solution.py:195
  102.9 6.3 %copy-start.27 = (u32[128]{0:T(128)S(1)}, u32[128]{0:T(128)}, u32[]{:S(2)}) copy-start(u32[128]{0:T(128)} %constant.153) | copy-start | bytes 1540
  104.6 23.6 %all-to-all-start.1 = ((f32[128,4,128,4]{2,3,1,0:T(4,128)}), f32[128,4,128,4]{2,3,1,0:T(4,128)S(1)}, u32[]{:S(2)}, u32[]{:S(2)}) async-start(f32[128,4,128,4]{2,3,1,0:T(4,128)} %copy.74), calls=%async_computation.1 | async-start | bytes 2097152 | tf_op jit(solution)/shard_map/all_to_all | solution.py:205
  128.3 16.1 %copy-start.3 = (f32[2,6,130,512]{3,2,1,0:T(8,128)S(1)}, f32[2,6,130,512]{3,2,1,0:T(8,128)}, u32[]{:S(2)}) copy-start(f32[2,6,130,512]{3,2,1,0:T(8,128)} %copy-done.2) | copy-start | bytes 9584644
  134.2 11.6 %collective-permute-start.4 = (f32[1,128,512]{2,1,0:T(8,128)S(1)}, f32[1,128,512]{2,1,0:T(8,128)S(1)}, u32[]{:S(2)}, u32[]{:S(2)}) collective-permute-start(f32[1,128,512]{2,1,0:T(8,128)S(1)} %get-tuple-element.48), channel_id=1, source_target_pairs={{4,0},{8,4},{12,8},{16,12},{20,16},{24,20},{28,24},{32,28},{36,32}... | collective-permute-start | bytes 786440 | tf_op jit(solution)/shard_map/ppermute | solution.py:30
  135.5 10.3 %collective-permute-start.5 = (f32[1,128,512]{2,1,0:T(8,128)S(1)}, f32[1,128,512]{2,1,0:T(8,128)S(1)}, u32[]{:S(2)}, u32[]{:S(2)}) collective-permute-start(f32[1,128,512]{2,1,0:T(8,128)S(1)} %get-tuple-element.47), channel_id=1, source_target_pairs={{0,4},{4,8},{8,12},{12,16},{16,20},{20,24},{24,28},{28,32},{32,36}... | collective-permute-start | bytes 786440 | tf_op jit(solution)/shard_map/ppermute | solution.py:29
  138.6 6.5 %collective-permute-start.6 = (f32[4,1,512]{2,1,0:T(1,128)S(1)}, f32[4,1,512]{2,1,0:T(1,128)S(1)}, u32[]{:S(2)}, u32[]{:S(2)}) collective-permute-start(f32[4,1,512]{2,1,0:T(1,128)S(1)} %get-tuple-element.50), channel_id=1, source_target_pairs={{1,0},{2,1},{3,2},{5,4},{6,5},{7,6},{9,8},{10,9},{11,10},{13,12},{... | collective-permute-start | bytes 24584 | tf_op jit(solution)/shard_map/ppermute | solution.py:30
  139.9 5.9 %collective-permute-start.7 = (f32[4,1,512]{2,1,0:T(1,128)S(1)}, f32[4,1,512]{2,1,0:T(1,128)S(1)}, u32[]{:S(2)}, u32[]{:S(2)}) collective-permute-start(f32[4,1,512]{2,1,0:T(1,128)S(1)} %get-tuple-element.49), channel_id=1, source_target_pairs={{0,1},{1,2},{2,3},{4,5},{5,6},{6,7},{8,9},{9,10},{10,11},{12,13},{... | collective-permute-start | bytes 24584 | tf_op jit(solution)/shard_map/ppermute | solution.py:29
  145.1 1.5 copy-start.18
  146.6 10.3 %copy-start.26 = (u32[128]{0:T(128)S(1)}, u32[128]{0:T(128)}, u32[]{:S(2)}) copy-start(u32[128]{0:T(128)} %constant.158) | copy-start | bytes 1540
  146.6 24.6 %copy-start.25 = (u32[128]{0:T(128)S(1)}, u32[128]{0:T(128)}, u32[]{:S(2)}) copy-start(u32[128]{0:T(128)} %constant.163) | copy-start | bytes 1540
  146.6 37.4 %copy-start.24 = (u32[128]{0:T(128)S(1)}, u32[128]{0:T(128)}, u32[]{:S(2)}) copy-start(u32[128]{0:T(128)} %constant.168) | copy-start | bytes 1540
  205.6 72.5 %copy-start.19 = (f32[4,128,512]{2,1,0:T(8,128)}, f32[4,128,512]{2,1,0:T(8,128)S(1)}, u32[]{:S(2)}) copy-start(f32[4,128,512]{2,1,0:T(8,128)S(1)} %multiply_subtract_fusion.2) | copy-start | bytes 3145732
  322.2 13.0 %copy-start.13 = (f32[4,128,512]{2,1,0:T(8,128)S(1)}, f32[4,128,512]{2,1,0:T(8,128)}, u32[]{:S(2)}) copy-start(f32[4,128,512]{2,1,0:T(8,128)} %get-tuple-element.22) | copy-start | bytes 3145732
  322.3 13.0 %copy-start.15 = (f32[4,128,512]{2,1,0:T(8,128)S(1)}, f32[4,128,512]{2,1,0:T(8,128)}, u32[]{:S(2)}) copy-start(f32[4,128,512]{2,1,0:T(8,128)} %get-tuple-element.23) | copy-start | bytes 3145732
  322.5 12.7 %copy-start.11 = (f32[4,128,512]{2,1,0:T(8,128)S(1)}, f32[4,128,512]{2,1,0:T(8,128)}, u32[]{:S(2)}) copy-start(f32[4,128,512]{2,1,0:T(8,128)} %get-tuple-element.21) | copy-start | bytes 3145732
  322.6 12.7 %copy-start.5 = (f32[4,128,512]{2,1,0:T(8,128)S(1)}, f32[4,128,512]{2,1,0:T(8,128)}, u32[]{:S(2)}) copy-start(f32[4,128,512]{2,1,0:T(8,128)} %get-tuple-element.18) | copy-start | bytes 3145732
  322.6 12.7 %copy-start.7 = (f32[4,128,512]{2,1,0:T(8,128)S(1)}, f32[4,128,512]{2,1,0:T(8,128)}, u32[]{:S(2)}) copy-start(f32[4,128,512]{2,1,0:T(8,128)} %get-tuple-element.19) | copy-start | bytes 3145732
  322.6 12.7 %copy-start.9 = (f32[4,128,512]{2,1,0:T(8,128)S(1)}, f32[4,128,512]{2,1,0:T(8,128)}, u32[]{:S(2)}) copy-start(f32[4,128,512]{2,1,0:T(8,128)} %get-tuple-element.20) | copy-start | bytes 3145732
  322.6 11.9 %collective-permute-start.8 = (f32[1,128,512]{2,1,0:T(8,128)S(1)}, f32[1,128,512]{2,1,0:T(8,128)S(1)}, u32[]{:S(2)}, u32[]{:S(2)}) collective-permute-start(f32[1,128,512]{2,1,0:T(8,128)S(1)} %get-tuple-element.44), channel_id=1, source_target_pairs={{4,0},{8,4},{12,8},{16,12},{20,16},{24,20},{28,24},{32,28},{36,32}... | collective-permute-start | bytes 786440 | tf_op jit(solution)/shard_map/ppermute | solution.py:30
  324.1 10.3 %collective-permute-start.9 = (f32[1,128,512]{2,1,0:T(8,128)S(1)}, f32[1,128,512]{2,1,0:T(8,128)S(1)}, u32[]{:S(2)}, u32[]{:S(2)}) collective-permute-start(f32[1,128,512]{2,1,0:T(8,128)S(1)} %get-tuple-element.43), channel_id=1, source_target_pairs={{0,4},{4,8},{8,12},{12,16},{16,20},{20,24},{24,28},{28,32},{32,36}... | collective-permute-start | bytes 786440 | tf_op jit(solution)/shard_map/ppermute | solution.py:29
  327.2 5.9 %collective-permute-start.10 = (f32[4,1,512]{2,1,0:T(1,128)S(1)}, f32[4,1,512]{2,1,0:T(1,128)S(1)}, u32[]{:S(2)}, u32[]{:S(2)}) collective-permute-start(f32[4,1,512]{2,1,0:T(1,128)S(1)} %get-tuple-element.46), channel_id=1, source_target_pairs={{1,0},{2,1},{3,2},{5,4},{6,5},{7,6},{9,8},{10,9},{11,10},{13,12},{... | collective-permute-start | bytes 24584 | tf_op jit(solution)/shard_map/ppermute | solution.py:30
  328.5 5.9 %collective-permute-start.11 = (f32[4,1,512]{2,1,0:T(1,128)S(1)}, f32[4,1,512]{2,1,0:T(1,128)S(1)}, u32[]{:S(2)}, u32[]{:S(2)}) collective-permute-start(f32[4,1,512]{2,1,0:T(1,128)S(1)} %get-tuple-element.45), channel_id=1, source_target_pairs={{0,1},{1,2},{2,3},{4,5},{5,6},{6,7},{8,9},{9,10},{10,11},{12,13},{... | collective-permute-start | bytes 24584 | tf_op jit(solution)/shard_map/ppermute | solution.py:29
  379.0 1.0 copy-start.20
  428.9 23.2 %copy-start.21 = (f32[4,128,512]{2,1,0:T(8,128)S(1)}, f32[4,128,512]{2,1,0:T(8,128)}, u32[]{:S(2)}) copy-start(f32[4,128,512]{2,1,0:T(8,128)} %copy-done.20) | copy-start | bytes 3145732
  496.8 14.3 %copy-start.14 = (f32[4,128,512]{2,1,0:T(8,128)S(1)}, f32[4,128,512]{2,1,0:T(8,128)}, u32[]{:S(2)}) copy-start(f32[4,128,512]{2,1,0:T(8,128)} %get-tuple-element.22) | copy-start | bytes 3145732
  496.8 14.3 %copy-start.16 = (f32[4,128,512]{2,1,0:T(8,128)S(1)}, f32[4,128,512]{2,1,0:T(8,128)}, u32[]{:S(2)}) copy-start(f32[4,128,512]{2,1,0:T(8,128)} %get-tuple-element.23) | copy-start | bytes 3145732
  498.4 12.7 %copy-start.12 = (f32[4,128,512]{2,1,0:T(8,128)S(1)}, f32[4,128,512]{2,1,0:T(8,128)}, u32[]{:S(2)}) copy-start(f32[4,128,512]{2,1,0:T(8,128)} %get-tuple-element.21) | copy-start | bytes 3145732
  498.5 12.7 %copy-start.6 = (f32[4,128,512]{2,1,0:T(8,128)S(1)}, f32[4,128,512]{2,1,0:T(8,128)}, u32[]{:S(2)}) copy-start(f32[4,128,512]{2,1,0:T(8,128)} %get-tuple-element.18) | copy-start | bytes 3145732
  498.5 12.7 %copy-start.8 = (f32[4,128,512]{2,1,0:T(8,128)S(1)}, f32[4,128,512]{2,1,0:T(8,128)}, u32[]{:S(2)}) copy-start(f32[4,128,512]{2,1,0:T(8,128)} %get-tuple-element.19) | copy-start | bytes 3145732
  498.5 12.7 %copy-start.10 = (f32[4,128,512]{2,1,0:T(8,128)S(1)}, f32[4,128,512]{2,1,0:T(8,128)}, u32[]{:S(2)}) copy-start(f32[4,128,512]{2,1,0:T(8,128)} %get-tuple-element.20) | copy-start | bytes 3145732
  498.5 11.9 %collective-permute-start.12 = (f32[1,128,512]{2,1,0:T(8,128)S(1)}, f32[1,128,512]{2,1,0:T(8,128)S(1)}, u32[]{:S(2)}, u32[]{:S(2)}) collective-permute-start(f32[1,128,512]{2,1,0:T(8,128)S(1)} %get-tuple-element.40), channel_id=1, source_target_pairs={{4,0},{8,4},{12,8},{16,12},{20,16},{24,20},{28,24},{32,28},{36,32}... | collective-permute-start | bytes 786440 | tf_op jit(solution)/shard_map/ppermute | solution.py:30
  500.1 10.3 %collective-permute-start.13 = (f32[1,128,512]{2,1,0:T(8,128)S(1)}, f32[1,128,512]{2,1,0:T(8,128)S(1)}, u32[]{:S(2)}, u32[]{:S(2)}) collective-permute-start(f32[1,128,512]{2,1,0:T(8,128)S(1)} %get-tuple-element.39), channel_id=1, source_target_pairs={{0,4},{4,8},{8,12},{12,16},{16,20},{20,24},{24,28},{28,32},{32,36}... | collective-permute-start | bytes 786440 | tf_op jit(solution)/shard_map/ppermute | solution.py:29
  503.1 5.9 %collective-permute-start.14 = (f32[4,1,512]{2,1,0:T(1,128)S(1)}, f32[4,1,512]{2,1,0:T(1,128)S(1)}, u32[]{:S(2)}, u32[]{:S(2)}) collective-permute-start(f32[4,1,512]{2,1,0:T(1,128)S(1)} %get-tuple-element.42), channel_id=1, source_target_pairs={{1,0},{2,1},{3,2},{5,4},{6,5},{7,6},{9,8},{10,9},{11,10},{13,12},{... | collective-permute-start | bytes 24584 | tf_op jit(solution)/shard_map/ppermute | solution.py:30
  504.4 5.9 %collective-permute-start.15 = (f32[4,1,512]{2,1,0:T(1,128)S(1)}, f32[4,1,512]{2,1,0:T(1,128)S(1)}, u32[]{:S(2)}, u32[]{:S(2)}) collective-permute-start(f32[4,1,512]{2,1,0:T(1,128)S(1)} %get-tuple-element.41), channel_id=1, source_target_pairs={{0,1},{1,2},{2,3},{4,5},{5,6},{6,7},{8,9},{9,10},{10,11},{12,13},{... | collective-permute-start | bytes 24584 | tf_op jit(solution)/shard_map/ppermute | solution.py:29
  554.7 3.5 copy-start.1
